TPU v7x, 1024 devices: a whole 8x8x8 slice. The times are simulated.
1024 devices in a mesh: pipe: 8 (over z), expert: 32 (over y, x_lo, core), dp: 4 (over x_hi).
Axes of the slice: x: 8 (x_hi: 4, x_lo: 2; x = x_hi * 2 + x_lo), y: 8, z: 8, core: 2. Of those that a mesh axis runs over, the one named last changes fastest.
Arguments:
- tokens: bfloat16 [8, 4096, 3584], P('pipe', 'expert', 'dp'), may hold values from -6 to 6
- expert_ids: int32 [8, 4096, 2], P('pipe', 'expert'), may hold values from 0 to 31, all different within a row; in each aligned block of 128 rows (0 to 127, 128 to 255, ..., all dimensions but the last counted through in order) at most 16 rows name the same one
- gate_levels: int32 [8, 4096, 2], P('pipe', 'expert'), may hold values from 1 to 255
- gain: bfloat16 [3584], P('dp'), may hold values from 0.5 to 2
- w_gate: bfloat16 [32, 3584, 1024], P('expert', None, 'dp'), may hold values from -0.09375 to 0.09375
- w_up: bfloat16 [32, 3584, 1024], P('expert', None, 'dp'), may hold values from -0.09375 to 0.09375
- w_down: bfloat16 [32, 1024, 3584], P('expert', 'dp'), may hold values from -0.1875 to 0.1875
Outputs:
- next_input: bfloat16 [8, 4096, 3584], P('pipe', 'expert', 'dp')
Inputs may be any that keep to these rules, and one draw needn't show every extreme that they name: `expert_ids`: each token names 2 different experts. Within each aligned block of 128 tokens of a section, no expert is named by more than 16 tokens, and in every draw some expert is named by exactly 16 tokens of some block.
All inputs are finite; a program needn't handle non-finite values.
Results may differ from a plain program's by a relative error of at most 0.012.
Values may be sent and summed in bfloat16 or wider, within the bound.
A program may use at most 32 MiB of HBM per device.

v0:
```python
import jax
import jax.numpy as jnp
from jax import lax
from jax.sharding import PartitionSpec as P

epsilon = 1e-06


def from_behind(value, axis, by):
    size = lax.axis_size(axis)
    return lax.ppermute(value, axis, [(i, (i + by) % size) for i in range(size)])


def body(tokens, expert_ids, gate_levels, gain, w_gate, w_up, w_down):
    own_rows = tokens[0]
    choose = expert_ids[0]
    levels = gate_levels[0].astype(jnp.float32)
    weights_gate = w_gate[0]
    weights_up = w_up[0]
    weights_down = w_down[0]
    num_tokens = own_rows.shape[0]
    quarter = own_rows.shape[1]
    fanout = choose.shape[1]
    experts = lax.axis_size("expert") * w_gate.shape[0]
    capacity = min(num_tokens, max(2, 2 * num_tokens * fanout // experts))
    full_width = weights_gate.shape[0]
    expert_iota = jnp.arange(experts, dtype=jnp.int32)
    matches = (choose[:, :, None] == expert_iota[None, None, :]).astype(jnp.int32)
    member = jnp.sum(matches, axis=1)
    before = jnp.cumsum(member, axis=0) - member
    slot_iota = jnp.arange(capacity, dtype=jnp.int32)
    placed = (member.T[:, None, :] == 1) & (before.T[:, None, :] == slot_iota[None, :, None])
    placed = placed.reshape(experts * capacity, num_tokens)
    outgoing = jnp.dot(placed.astype(jnp.bfloat16), own_rows, preferred_element_type=jnp.float32)
    outgoing = outgoing.astype(jnp.bfloat16).reshape(experts, capacity, quarter)
    slot_of = jnp.sum(
        matches * (expert_iota[None, None, :] * capacity + before[:, None, :]), axis=2
    )
    shares = levels / jnp.sum(levels, axis=1, keepdims=True)
    gain_row = gain[None, :]
    arrived = lax.all_to_all(outgoing, "expert", split_axis=0, concat_axis=0, tiled=True)
    sources = arrived.shape[0]
    slot_count = arrived.shape[1]
    flat_rows = arrived.reshape(sources * slot_count, quarter)
    portion = (
        lax.all_gather(flat_rows, "dp", axis=1, tiled=True),
        lax.all_gather(gain_row, "dp", axis=1, tiled=True),
    )
    part_rows = portion[0]
    part_gain = portion[1]
    scaled = (part_rows.astype(jnp.float32) * part_gain.astype(jnp.float32)).astype(jnp.bfloat16)
    gate_acc = jnp.dot(scaled, weights_gate, preferred_element_type=jnp.float32)
    up_acc = jnp.dot(scaled, weights_up, preferred_element_type=jnp.float32)
    gate_acc, up_acc = (gate_acc, up_acc)
    squares = jnp.sum(jnp.square(portion[0].astype(jnp.float32)), axis=1)
    gate_acc, up_acc, squares = (gate_acc, up_acc, squares)
    inverse = lax.rsqrt(squares / full_width + epsilon)
    gate_value = inverse[:, None] * gate_acc
    up_value = inverse[:, None] * up_acc
    hidden = (jax.nn.silu(gate_value) * up_value).astype(jnp.bfloat16)
    summed = lax.psum_scatter(
        lax.dot_general(
            weights_down, hidden, (((0,), (1,)), ((), ())), preferred_element_type=jnp.float32
        ).astype(jnp.bfloat16),
        "dp",
        scatter_dimension=0,
        tiled=True,
    )
    result = summed.reshape(quarter, sources, slot_count)
    returned_rows = lax.all_to_all(result, "expert", split_axis=1, concat_axis=1, tiled=True)
    flat_back = returned_rows.reshape(quarter, experts * capacity)
    every_slot = jnp.arange(experts * capacity, dtype=jnp.int32)
    combined = own_rows.astype(jnp.float32)
    for slot_pick in range(fanout):
        selector = (slot_of[:, slot_pick, None] == every_slot[None, :]).astype(jnp.bfloat16)
        picked = lax.dot_general(
            selector, flat_back, (((1,), (1,)), ((), ())), preferred_element_type=jnp.float32
        )
        combined = combined + shares[:, slot_pick, None] * picked
    layer_out = combined.astype(jnp.bfloat16)
    shifted = from_behind(layer_out, "pipe", 1)
    return shifted[None]


def solution(mesh):
    return jax.shard_map(
        body,
        mesh=mesh,
        in_specs=(
            P("pipe", "expert", "dp"),
            P("pipe", "expert", None),
            P("pipe", "expert", None),
            P("dp"),
            P("expert", None, "dp"),
            P("expert", None, "dp"),
            P("expert", "dp", None),
        ),
        out_specs=P("pipe", "expert", "dp"),
        check_vma=False,
    )
```

profile of v0, /device:TPU:2, one launch (start us, length us, event | category | flops | bytes accessed | tf_op | source)
XLA Modules:
  0.0 289.7 jit_solution(6250504348125079448)
XLA Ops:
  6.5 0.0 copy-start
  6.5 0.0 all-gather.4.cloned.1.call-start
  6.5 0.8 convert_reduce_fusion
  7.4 0.1 copy.14
  7.5 0.2 reduce_window_sum.11
  7.7 0.1 copy.17
  7.7 0.1 fusion.44
  7.8 1.3 convolution_convert_fusion.1
  9.1 42.7 %all_to_all.10 = bf16[32,16,896]{2,1,0:T(8,128)(2,1)} all-to-all(bf16[32,16,896]{2,1,0:T(8,128)(2,1)S(1)} %bitcast.54), channel_id=1, replica_groups=mesh['pipe'=8,'expert'=32,'dp'=4] {'expert'}, dimensions={0} | all-to-all | bytes 1835008 | tf_op jit(solution)/shard_map/all_to_all | solution.py:41
  51.9 0.0 all-gather.4.cloned.1.call-update
  51.9 0.0 reduce-scatter.4.cloned.1.call-start
  51.9 0.0 copy-done.4
  52.0 13.7 %all-gather.1 = bf16[4,1,896]{2,1,0:T(2,128)(2,1)S(1)} all-gather(bf16[1,1,896]{2,1,0:T(2,128)(2,1)S(1)} %reshape.94), channel_id=2, replica_groups=mesh['pipe'=8,'expert'=32,'dp'=4] {'dp'}, dimensions={0}, use_global_device_ids=true | all-gather | bytes 8960 | tf_op jit(solution)/shard_map/all_gather | solution.py:47
  65.8 64.8 %all-gather.4.cloned.1.call-done = bf16[512,3584]{1,0:T(8,128)(2,1)} async-done(((bf16[512,896]{1,0:T(8,128)(2,1)}), bf16[512,3584]{1,0:T(8,128)(2,1)}) %all-gather.4.cloned.1.call-update) | async-done | bytes 3670032 | tf_op jit(solution)/shard_map/all_gather | solution.py:46
  130.6 3.0 %fusion = f32[512]{0:T(512)S(1)} fusion(bf16[512,3584]{1,0:T(8,128)(2,1)} %all-gather.4.cloned.1.call-done), kind=kLoop, calls=%fused_computation.2 | loop fusion | flops 5504512 | bytes 3672064 | tf_op jit(solution)/shard_map/reduce_sum | solution.py:55
  133.6 0.2 copy-done.1
  133.8 2.6 fusion.10
  136.4 0.0 copy-done
  136.4 8.4 %fusion.2 = bf16[3584,512]{0,1:T(8,128)(2,1)} fusion(bf16[1,256,3584]{2,1,0:T(8,128)(2,1)S(1)} %copy-done, bf16[1,3584,256]{2,1,0:T(8,128)(2,1)} %param.12, bf16[512,3584]{1,0:T(8,128)(2,1)} %all-gather.4.cloned.1.call-done, f32[3584]{0:T(1024)S(1)} %reshape.96, f32[512,256]{1,0:T(8,128)S(1)} %fusion.10, f32[512]{0:T(512)S(1)} %add_rsqrt_fusion), kind=kOutput, calls=%fused_computation.5 | convolution fusion | flops 1887305728 | bytes 11550720 | tf_op jit(solution)/shard_map/dot_general | solution.py:62
  144.8 5.9 %copy.18 = bf16[3584,512]{1,0:T(8,128)(2,1)} copy(bf16[3584,512]{0,1:T(8,128)(2,1)} %fusion.2) | data formatting | bytes 7340032
  150.7 0.0 reduce-scatter.4.cloned.1.call-update
  150.7 81.0 %reduce-scatter.4.cloned.1.call-done = bf16[896,512]{1,0:T(8,128)(2,1)} async-done(((bf16[3584,512]{1,0:T(8,128)(2,1)}), bf16[896,512]{1,0:T(8,128)(2,1)}) %reduce-scatter.4.cloned.1.call-update) | async-done | bytes 917520
  231.7 2.2 copy.19
  233.9 8.4 %all-to-all-start.1 = ((bf16[896,32,16]{0,2,1:T(8,128)(2,1)}), bf16[896,32,16]{0,2,1:T(8,128)(2,1)S(1)}, u32[]{:S(2)}, u32[]{:S(2)}) async-start(bf16[896,32,16]{0,2,1:T(8,128)(2,1)} %bitcast.52), calls=%async_computation.1 | async-start | bytes 1835008 | tf_op jit(solution)/shard_map/all_to_all | solution.py:70
  242.4 0.1 copy.16
  242.5 26.0 %all-to-all-done.1 = bf16[896,32,16]{0,2,1:T(8,128)(2,1)S(1)} async-done(((bf16[896,32,16]{0,2,1:T(8,128)(2,1)}), bf16[896,32,16]{0,2,1:T(8,128)(2,1)S(1)}, u32[]{:S(2)}, u32[]{:S(2)}) %all-to-all-start.1) | async-done | bytes 917536 | tf_op jit(solution)/shard_map/all_to_all | solution.py:70
  268.5 0.0 copy-done.2
  268.5 0.4 fusion.26
  268.9 0.4 fusion.32
  269.2 3.7 %collective-permute-start = (bf16[128,896]{1,0:T(8,128)(2,1)S(1)}, bf16[128,896]{1,0:T(8,128)(2,1)S(1)}, u32[]{:S(2)}, u32[]{:S(2)}) collective-permute-start(bf16[128,896]{1,0:T(8,128)(2,1)S(1)} %fusion.32), channel_id=1, source_target_pairs={{0,128},{128,256},{256,384},{384,512},{512,640},{640,768},{768,896... | collective-permute-start | bytes 688136 | tf_op jit(solution)/shard_map/ppermute | solution.py:11
  273.0 9.2 %collective-permute-done = bf16[128,896]{1,0:T(8,128)(2,1)S(1)} collective-permute-done((bf16[128,896]{1,0:T(8,128)(2,1)S(1)}, bf16[128,896]{1,0:T(8,128)(2,1)S(1)}, u32[]{:S(2)}, u32[]{:S(2)}) %collective-permute-start) | collective-permute-done | bytes 229408 | tf_op jit(solution)/shard_map/ppermute | solution.py:11
  282.2 0.7 copy.21
  (19 shorter events, 0.2 us)
Async XLA Ops:
  6.5 129.9 %copy-start = (bf16[1,256,3584]{2,1,0:T(8,128)(2,1)S(1)}, bf16[1,256,3584]{2,1,0:T(8,128)(2,1)}, u32[]{:S(2)}) copy-start(bf16[1,256,3584]{2,1,0:T(8,128)(2,1)} %param.13) | copy-start | bytes 5505028
  6.5 45.4 %copy-start.4 = (bf16[896]{0:T(1024)(128)(2,1)S(1)}, bf16[896]{0:T(1024)(128)(2,1)}, u32[]{:S(2)}) copy-start(bf16[896]{0:T(1024)(128)(2,1)} %param.10) | copy-start | bytes 5380
  6.5 124.1 %all-gather.4.cloned.1.call-start = ((), (), s32[]{:S(2)}) async-start(), calls=%async_computation.3 | async-start | bytes 4587520 | tf_op jit(solution)/shard_map/all_gather | solution.py:46
  51.9 179.8 %reduce-scatter.4.cloned.1.call-start = ((), (), s32[]{:S(2)}) async-start(), calls=%async_computation.4 | async-start | bytes 4587520
  130.6 3.1 %copy-start.1 = (bf16[512,3584]{1,0:T(8,128)(2,1)S(1)}, bf16[512,3584]{1,0:T(8,128)(2,1)}, u32[]{:S(2)}) copy-start(bf16[512,3584]{1,0:T(8,128)(2,1)} %all-gather.4.cloned.1.call-done) | copy-start | bytes 11010052
  150.7 91.7 %copy-start.5 = (s32[1,128,2]{1,2,0:T(2,128)S(1)}, s32[1,128,2]{1,2,0:T(2,128)}, u32[]{:S(2)}) copy-start(s32[1,128,2]{1,2,0:T(2,128)} %param.9) | copy-start | bytes 3076
  150.7 91.8 %copy-start.3 = (s32[1,128,2]{1,2,0:T(2,128)S(1)}, s32[1,128,2]{1,2,0:T(2,128)}, u32[]{:S(2)}) copy-start(s32[1,128,2]{1,2,0:T(2,128)} %param.8) | copy-start | bytes 3076
  150.7 117.8 %copy-start.2 = (bf16[1,128,896]{2,1,0:T(8,128)(2,1)S(1)}, bf16[1,128,896]{2,1,0:T(8,128)(2,1)}, u32[]{:S(2)}) copy-start(bf16[1,128,896]{2,1,0:T(8,128)(2,1)} %param.7) | copy-start | bytes 688132
  233.9 34.6 %all-to-all-start.1 = ((bf16[896,32,16]{0,2,1:T(8,128)(2,1)}), bf16[896,32,16]{0,2,1:T(8,128)(2,1)S(1)}, u32[]{:S(2)}, u32[]{:S(2)}) async-start(bf16[896,32,16]{0,2,1:T(8,128)(2,1)} %bitcast.52), calls=%async_computation.1 | async-start | bytes 1835008 | tf_op jit(solution)/shard_map/all_to_all | solution.py:70
  269.2 12.9 %collective-permute-start = (bf16[128,896]{1,0:T(8,128)(2,1)S(1)}, bf16[128,896]{1,0:T(8,128)(2,1)S(1)}, u32[]{:S(2)}, u32[]{:S(2)}) collective-permute-start(bf16[128,896]{1,0:T(8,128)(2,1)S(1)} %fusion.32), channel_id=1, source_target_pairs={{0,128},{128,256},{256,384},{384,512},{512,640},{640,768},{768,896... | collective-permute-start | bytes 688136 | tf_op jit(solution)/shard_map/ppermute | solution.py:11
Sparse Core Ops, SparseCore 0:
  52.0 78.5 all-gather.3
  150.9 80.7 reduce-scatter.3
where the time goes:
time: 290 us
  waiting for transfers between devices  181 us (62%)
  blocking collectives  56.5 us (19%)
  between operations  13.5 us (5%)
  matrix products  13.1 us (5%)
  starting transfers between devices  12.2 us (4%)
  local copies, waits for them, and re-layouts  9.24 us (3%)
  other arithmetic  4.19 us (1%)
    unnamed x3, waiting for transfers between devices  81 us
    all_gather x1, waiting for transfers between devices, body(): lax.all_gather(flat_rows, 'dp', axis=1, tiled=True)  64.8 us
    all_to_all x1, blocking collectives, body(): lax.all_to_all(outgoing, 'expert', split_axis=0, concat_axis=0, tiled=True)  42.7 us
    all_to_all x1, waiting for transfers between devices, body(): lax.all_to_all(result, 'expert', split_axis=1, concat_axis=1, tiled=True)  26 us
    all_gather x1, blocking collectives, body(): lax.all_gather(gain_row, 'dp', axis=1, tiled=True)  13.7 us
    ppermute x1, waiting for transfers between devices, from_behind(): lax.ppermute(value, axis, [(i, (i + by) % size) for i in range(size)])  9.2 us
    unnamed x16, local copies, waits for them, and re-layouts  9.01 us
    all_to_all x1, starting transfers between devices, body(): lax.all_to_all(result, 'expert', split_axis=1, concat_axis=1, tiled=True)  8.45 us
  transfers between devices with their start and end apart: 4, of which 4 were waited for; matrix products, arithmetic and copies ran while one was open for 0% of the time, Pallas kernels for 0%

commit v1 on v0

v1 whole, which is shorter than its diff:
```python
import functools

import jax
import jax.numpy as jnp
from jax import lax
from jax.experimental import pallas as pl
from jax.experimental.pallas import tpu as pltpu
from jax.sharding import PartitionSpec as P

MESH = pl.DeviceIdType.MESH
epsilon = 1e-06
bf16 = jnp.bfloat16
f32 = jnp.float32


def kernel(sizes, cap, ids_ref, lev_ref, tok_ref, gain_ref, wg_any, wu_any, wd_any, out_ref,
           wg, wu, wd, meta, meta_nb, meta_prev, meta_pnb, tok_nb, tok_prev, outb, gat, gains,
           part, rs_opp, rs_l, rs_r, res, ret, xp_out, xp_in,
           w_sem, disp_s, disp_r, ag_s, ag_r, rs_s, rs_rr, ret_s, ret_r, misc_s, misc_r):
    n_pipe, n_exp, n_dp = sizes
    group = n_exp // 2
    tokens, quarter = tok_ref.shape
    half_rows = group * cap
    chunk = half_rows // 2
    split = chunk // 2
    full_width = n_dp * quarter

    z = lax.axis_index("pipe")
    e = lax.axis_index("expert")
    d = lax.axis_index("dp")
    x_lo = lax.rem(lax.div(e, 2), 2)
    g = lax.div(e, 4) * 2 + lax.rem(e, 2)
    right, left = lax.rem(d + 1, n_dp), lax.rem(d + n_dp - 1, n_dp)
    z_next, z_prev = lax.rem(z + 1, n_pipe), lax.rem(z + n_pipe - 1, n_pipe)

    def member(i):
        return lax.div(i, 2) * 4 + x_lo * 2 + lax.rem(i, 2)

    def offset(s):
        return jnp.where(lax.rem(s, 2) == 1, lax.div(s + 1, 2), group - lax.div(s, 2))

    def ahead(s):
        return member(lax.rem(g + offset(s), group))

    def behind(s):
        return member(lax.rem(g + 2 * group - offset(s), group))

    across = lax.div(e, 4) * 4 + (1 - x_lo) * 2 + lax.rem(e, 2)

    barrier = pltpu.get_barrier_semaphore()

    def tell_group(s, carry):
        pl.semaphore_signal(barrier, inc=1, device_id=(z, ahead(s), d), device_id_type=MESH)
        return carry

    def tell_before(s, carry):
        pl.semaphore_signal(barrier, inc=1, device_id=(z_prev, ahead(s), d), device_id_type=MESH)
        return carry

    pl.semaphore_signal(barrier, inc=1, device_id=(z, across, d), device_id_type=MESH)
    pl.semaphore_signal(barrier, inc=1, device_id=(z, e, right), device_id_type=MESH)
    pl.semaphore_signal(barrier, inc=1, device_id=(z, e, left), device_id_type=MESH)
    lax.fori_loop(1, group, tell_group, 0)
    lax.fori_loop(0, group, tell_before, 0)

    quarters = [d, left, right, lax.rem(d + 2, n_dp)]
    loads = []
    for q in range(4):
        at = pl.ds(pl.multiple_of(quarters[q] * quarter, 128), quarter)
        loads.append(pltpu.make_async_copy(wg_any.at[at, :], wg.at[q], w_sem.at[3 * q]))
        loads.append(pltpu.make_async_copy(wu_any.at[at, :], wu.at[q], w_sem.at[3 * q + 1]))
        loads.append(pltpu.make_async_copy(wd_any.at[:, at], wd.at[q], w_sem.at[3 * q + 2]))
    for copy in loads:
        copy.start()

    def slots(meta_ref):
        i = lax.broadcasted_iota(jnp.int32, (group, tokens), 0)
        off = jnp.where((i & 1) == 1, (i + 1) >> 1, group - (i >> 1))
        return i, off

    def place(meta_ref, sign):
        i, off = slots(meta_ref)
        member_of = (g + 2 * group + sign * off) & (group - 1)
        expert = (member_of >> 1) * 4 + x_lo * 2 + (member_of & 1)
        first = meta_ref[0:1, :] == expert
        second = meta_ref[1:2, :] == expert
        named = jnp.where(first | second, 1.0, 0.0)
        before_of = lax.broadcasted_iota(jnp.int32, (tokens, tokens), 0) < lax.broadcasted_iota(jnp.int32, (tokens, tokens), 1)
        before = jnp.dot(named.astype(bf16), jnp.where(before_of, 1.0, 0.0).astype(bf16), preferred_element_type=f32)
        rank = jnp.where(named > 0.5, before, 255.0)
        spread = jnp.where(
            (lax.broadcasted_iota(jnp.int32, (half_rows, group), 0) // cap) == lax.broadcasted_iota(jnp.int32, (half_rows, group), 1), 1.0, 0.0
        ).astype(bf16)
        wide = jnp.dot(spread, rank.astype(bf16), preferred_element_type=f32)
        slot = lax.broadcasted_iota(jnp.int32, (half_rows, tokens), 0) & (cap - 1)
        return wide == slot.astype(f32), first, second, spread

    def route(meta_ref, token_ref, h):
        placed, _, _, _ = place(meta_ref, 1)
        rows = jnp.dot(jnp.where(placed, 1.0, 0.0).astype(bf16), token_ref[...], preferred_element_type=f32).astype(bf16)
        outb[h * half_rows:(h + 1) * half_rows, :] = rows
        gat[0, h * half_rows:h * half_rows + cap, :] = rows[0:cap]

    def rc(src, dst, ssem, rsem, device):
        return pltpu.make_async_remote_copy(src_ref=src, dst_ref=dst, send_sem=ssem, recv_sem=rsem, device_id=device, device_id_type=MESH)

    meta[0:2, :] = ids_ref[...]
    meta[2:4, :] = lev_ref[...]
    meta[4:8, :] = jnp.zeros((4, tokens), jnp.int32)
    gains[0] = jnp.broadcast_to(gain_ref[...].astype(f32), (16, quarter)).astype(bf16)
    route(meta, tok_ref, 0)

    pl.semaphore_wait(barrier, 2 * group + 2)

    nb = (z, across, d)
    to_right, to_left = (z, e, right), (z, e, left)
    copy_meta_nb = rc(meta, meta_nb, misc_s.at[0], misc_r.at[0], nb)
    copy_tok_nb = rc(tok_ref, tok_nb, misc_s.at[1], misc_r.at[1], nb)
    copy_meta_prev = rc(meta, meta_prev, misc_s.at[2], misc_r.at[2], (z_next, e, d))
    copy_tok_prev = rc(tok_ref, tok_prev, misc_s.at[3], misc_r.at[3], (z_next, e, d))
    copy_meta_pnb = rc(meta_prev, meta_pnb, misc_s.at[4], misc_r.at[4], nb)
    copy_gain_r = rc(gains.at[0], gains.at[1], misc_s.at[5], misc_r.at[5], to_right)
    copy_gain_l = rc(gains.at[0], gains.at[2], misc_s.at[6], misc_r.at[6], to_left)
    copy_gain_o = rc(gains.at[1], gains.at[3], misc_s.at[7], misc_r.at[7], to_right)
    copy_part = rc(xp_out, xp_in, misc_s.at[8], misc_r.at[8], nb)

    def dispatch(h, s):
        at = pl.ds(pl.multiple_of(h * half_rows + s * cap, cap), cap)
        return rc(outb.at[at, :], gat.at[0, at, :], disp_s.at[h, s], disp_r.at[h, s], (z, ahead(s), d))

    def giving_back(h, s):
        at = pl.ds(pl.multiple_of(h * half_rows + s * cap, cap), cap)
        return rc(res.at[at, :], ret.at[at, :], ret_s.at[h, s], ret_r.at[h, s], (z_next, behind(s), d))

    def each(low, high, action):
        def step(s, carry):
            action(s)
            return carry

        lax.fori_loop(low, high, step, 0)

    copy_meta_nb.start()
    copy_tok_nb.start()
    each(1, group, lambda s: dispatch(0, s).start())
    copy_gain_r.start()
    copy_gain_l.start()
    copy_meta_prev.start()

    chunks = [(0, 0), (1, 0), (1, group // 2), (0, group // 2)]
    starts = [h * half_rows + s * cap for h, s in chunks]

    def rows_of(c):
        return slice(starts[c], starts[c] + chunk)

    def upper(c):
        return slice(starts[c], starts[c] + split)

    def lower(c):
        return slice(starts[c] + split, starts[c] + chunk)

    def view(ref, q, at):
        return ref.at[q, pl.ds(at.start, at.stop - at.start), :]

    def flat(ref, at):
        return ref.at[pl.ds(at.start, at.stop - at.start), :]

    ag_r1 = [rc(view(gat, 0, rows_of(c)), view(gat, 1, rows_of(c)), ag_s.at[c, 0], ag_r.at[c, 0], to_right) for c in range(4)]
    ag_l1 = [rc(view(gat, 0, rows_of(c)), view(gat, 2, rows_of(c)), ag_s.at[c, 1], ag_r.at[c, 1], to_left) for c in range(4)]
    ag_r2 = [rc(view(gat, 1, upper(c)), view(gat, 3, upper(c)), ag_s.at[c, 2], ag_r.at[c, 2], to_right) for c in range(4)]
    ag_l2 = [rc(view(gat, 2, lower(c)), view(gat, 3, lower(c)), ag_s.at[c, 3], ag_r.at[c, 3], to_left) for c in range(4)]
    rs_r2 = [rc(view(part, 3, upper(c)), flat(rs_opp, upper(c)), rs_s.at[c, 0], rs_rr.at[c, 0], to_right) for c in range(4)]
    rs_l2 = [rc(view(part, 3, lower(c)), flat(rs_opp, lower(c)), rs_s.at[c, 1], rs_rr.at[c, 1], to_left) for c in range(4)]
    rs_r1 = [rc(view(part, 2, rows_of(c)), flat(rs_l, rows_of(c)), rs_s.at[c, 2], rs_rr.at[c, 2], to_right) for c in range(4)]
    rs_l1 = [rc(view(part, 1, rows_of(c)), flat(rs_r, rows_of(c)), rs_s.at[c, 3], rs_rr.at[c, 3], to_left) for c in range(4)]

    def gather(c):
        h, s0 = chunks[c]
        each(max(s0, 1), s0 + group // 2, lambda s: dispatch(h, s).wait_recv())
        ag_r1[c].start()
        ag_l1[c].start()

    def forward(c):
        ag_r1[c].wait_recv()
        ag_r2[c].start()
        ag_l1[c].wait_recv()
        ag_l2[c].start()

    def compute(c):
        at = rows_of(c)
        gate = jnp.zeros((chunk, wg.shape[2]), f32)
        up = jnp.zeros((chunk, wg.shape[2]), f32)
        squares = jnp.zeros((chunk, 1), f32)
        for q in range(4):
            if q == 3:
                ag_r2[c].wait_recv()
                ag_l2[c].wait_recv()
            wide = gat[q, at, :].astype(f32)
            squares = squares + jnp.sum(wide * wide, axis=1, keepdims=True)
            scaled = (wide * gains[q, 0:1, :].astype(f32)).astype(bf16)
            gate = gate + jnp.dot(scaled, wg[q], preferred_element_type=f32)
            up = up + jnp.dot(scaled, wu[q], preferred_element_type=f32)
        inverse = lax.rsqrt(squares / full_width + epsilon)
        gate = inverse * gate
        up = inverse * up
        hidden = (gate / (1.0 + jnp.exp(-gate)) * up).astype(bf16)
        part[3, at, :] = jnp.dot(hidden, wd[3], preferred_element_type=f32).astype(bf16)
        rs_r2[c].start()
        rs_l2[c].start()
        for q in (1, 2, 0):
            part[q, at, :] = jnp.dot(hidden, wd[q], preferred_element_type=f32).astype(bf16)

    def reduce_on(c):
        rs_r2[c].wait_recv()
        at = upper(c)
        part[2, at, :] = (part[2, at, :].astype(f32) + rs_opp[at, :].astype(f32)).astype(bf16)
        rs_r1[c].start()
        rs_l2[c].wait_recv()
        at = lower(c)
        part[1, at, :] = (part[1, at, :].astype(f32) + rs_opp[at, :].astype(f32)).astype(bf16)
        rs_l1[c].start()

    def give_back(c):
        at = rows_of(c)
        h, s0 = chunks[c]
        rs_r1[c].wait_recv()
        rs_l1[c].wait_recv()
        res[at, :] = (part[0, at, :].astype(f32) + rs_l[at, :].astype(f32) + rs_r[at, :].astype(f32)).astype(bf16)
        each(s0, s0 + group // 2, lambda s: giving_back(h, s).start())

    def combine(meta_ref, h):
        placed, first, second, spread = place(meta_ref, 1)
        levels = meta_ref[2:4, :].astype(f32)
        total = levels[0:1] + levels[1:2]
        share = jnp.where(first, levels[0:1] / total, jnp.where(second, levels[1:2] / total, 0.0))
        high = share.astype(bf16)
        low = (share - high.astype(f32)).astype(bf16)
        acc = jnp.zeros((tokens, quarter), f32)
        for piece in (high, low):
            weight = jnp.where(placed, jnp.dot(spread, piece, preferred_element_type=f32), 0.0).astype(bf16)
            acc = acc + lax.dot_general(
                weight, ret[h * half_rows:(h + 1) * half_rows, :], (((0,), (0,)), ((), ())), preferred_element_type=f32
            )
        return acc

    gather(0)
    copy_meta_nb.wait_recv()
    copy_tok_nb.wait_recv()
    route(meta_nb, tok_nb, 1)
    each(1, group, lambda s: dispatch(1, s).start())
    copy_tok_prev.start()
    gather(1)
    forward(0)
    copy_gain_r.wait_recv()
    copy_gain_o.start()
    gather(2)
    copy_meta_prev.wait_recv()
    copy_meta_pnb.start()
    gather(3)
    for copy in loads:
        copy.wait()
    copy_gain_l.wait_recv()
    copy_gain_o.wait_recv()
    compute(0)
    forward(1)
    reduce_on(0)
    compute(1)
    forward(2)
    give_back(0)
    reduce_on(1)
    compute(2)
    forward(3)
    give_back(1)
    reduce_on(2)
    compute(3)
    give_back(2)
    reduce_on(3)
    copy_meta_pnb.wait_recv()
    each(0, group, lambda s: giving_back(1, s).wait_recv())
    xp_out[...] = combine(meta_pnb, 1).astype(bf16)
    copy_part.start()
    give_back(3)
    copy_tok_prev.wait_recv()
    each(0, group, lambda s: giving_back(0, s).wait_recv())
    mine = combine(meta_prev, 0)
    copy_part.wait_recv()
    out_ref[...] = (tok_prev[...].astype(f32) + (mine + xp_in[...].astype(f32))).astype(bf16)

    for copy in (copy_meta_nb, copy_tok_nb, copy_meta_prev, copy_tok_prev, copy_meta_pnb, copy_gain_r, copy_gain_l, copy_gain_o, copy_part):
        copy.wait_send()
    for c in range(4):
        for copies in (ag_r1, ag_l1, ag_r2, ag_l2, rs_r2, rs_l2, rs_r1, rs_l1):
            copies[c].wait_send()
    for h in range(2):
        each(1, group, lambda s: dispatch(h, s).wait_send())
        each(0, group, lambda s: giving_back(h, s).wait_send())


def body(sizes, interpret, tokens, expert_ids, gate_levels, gain, w_gate, w_up, w_down):
    rows, quarter = tokens.shape[1:]
    fanout = expert_ids.shape[2]
    n_exp = sizes[1]
    cap = min(rows, max(2, 2 * rows * fanout // n_exp))
    group = n_exp // 2
    every = 2 * group * cap
    ff = w_gate.shape[2]
    vmem = pl.BlockSpec(memory_space=pltpu.VMEM)
    anywhere = pl.BlockSpec(memory_space=pl.ANY)
    dma = pltpu.SemaphoreType.DMA
    out = pl.pallas_call(
        functools.partial(kernel, sizes, cap),
        out_shape=jax.ShapeDtypeStruct((rows, quarter), bf16),
        in_specs=[vmem, vmem, vmem, vmem, anywhere, anywhere, anywhere],
        out_specs=vmem,
        scratch_shapes=[
            pltpu.VMEM((4, quarter, ff), bf16),
            pltpu.VMEM((4, quarter, ff), bf16),
            pltpu.VMEM((4, ff, quarter), bf16),
            *[pltpu.VMEM((8, rows), jnp.int32)] * 4,
            *[pltpu.VMEM((rows, quarter), bf16)] * 2,
            pltpu.VMEM((every, quarter), bf16),
            pltpu.VMEM((4, every, quarter), bf16),
            pltpu.VMEM((4, 16, quarter), bf16),
            pltpu.VMEM((4, every, quarter), bf16),
            *[pltpu.VMEM((every, quarter), bf16)] * 5,
            *[pltpu.VMEM((rows, quarter), bf16)] * 2,
            dma((12,)),
            dma((2, group)),
            dma((2, group)),
            dma((4, 4)),
            dma((4, 4)),
            dma((4, 4)),
            dma((4, 4)),
            dma((2, group)),
            dma((2, group)),
            dma((9,)),
            dma((9,)),
        ],
        compiler_params=pltpu.CompilerParams(collective_id=0, has_side_effects=True, vmem_limit_bytes=48 * 1024 * 1024),
        interpret=interpret,
    )(expert_ids[0].T, gate_levels[0].T, tokens[0], gain[None, :], w_gate[0], w_up[0], w_down[0])
    return out[None]


def solution(mesh, interpret=False):
    sizes = (mesh.shape["pipe"], mesh.shape["expert"], mesh.shape["dp"])
    return jax.shard_map(
        functools.partial(body, sizes, interpret),
        mesh=mesh,
        in_specs=(
            P("pipe", "expert", "dp"),
            P("pipe", "expert", None),
            P("pipe", "expert", None),
            P("dp"),
            P("expert", None, "dp"),
            P("expert", None, "dp"),
            P("expert", "dp", None),
        ),
        out_specs=P("pipe", "expert", "dp"),
        check_vma=False,
    )
```

time: 290 us -> 179 us (0.62)
  the two profiles are of different devices: /device:TPU:2 before, /device:TPU:6 now
where the time goes in v1:
time: 179 us
  Pallas kernels  171 us (96%)
  local copies, waits for them, and re-layouts  8.17 us (5%)
    pallas_call x1, Pallas kernels, body(): pl.pallas_call(functools.partial(kernel, sizes, cap), out_shape=jax.Shape...  171 us
    unnamed x13, local copies, waits for them, and re-layouts  7.48 us

profile of v1, /device:TPU:6, one launch (start us, length us, event | category | flops | bytes accessed | tf_op | source)
XLA Modules:
  0.0 178.7 jit_solution(16763071619885371953)
XLA Ops:
  0.0 0.7 broadcast_in_dim.6.gain_ref
  0.7 0.0 copy-start
  0.7 1.5 copy-done
  2.2 0.0 copy-start.1
  2.2 1.5 copy-done.1
  3.7 0.0 copy-start.2
  3.7 1.5 copy-done.2
  5.2 0.0 copy-start.3
  5.2 0.9 copy-done.3
  6.1 0.0 copy-start.4
  6.1 0.7 copy-done.4
  6.8 0.0 copy-start.5
  6.8 0.7 copy-done.5
  7.5 170.6 %shard_map.73 = bf16[128,896]{1,0:T(8,128)(2,1)S(1)} custom-call(s32[2,128]{1,0:T(2,128)S(1)} %bitcast.16, s32[2,128]{1,0:T(2,128)S(1)} %bitcast.17, bf16[128,896]{1,0:T(8,128)(2,1)S(1)} %bitcast.15, bf16[1,896]{1,0:T(2,128)(2,1)S(1)} %broadcast_in_dim.6.gain_ref, bf16[3584,256]{1,0:T(8,128)(2,1)S(1)} %bitcast.11, bf16[3584,256]{1,0:T(8,128)(2,1)S(1)} %bitcast.12, ...), custom_call_target="tpu_custom_call" | custom-call | tf_op jit(solution)/shard_map/pallas_call | solution.py:309
  178.0 0.7 copy.9
Async XLA Ops:
  0.7 1.5 copy-start
  2.2 1.5 copy-start.1
  3.7 1.5 copy-start.2
  5.2 0.9 copy-start.3
  6.1 0.7 copy-start.4
  6.8 0.7 copy-start.5

commit v2 on v1

v2 whole, which is shorter than its diff:
```python
import functools

import jax
import jax.numpy as jnp
from jax import lax
from jax.experimental import pallas as pl
from jax.experimental.pallas import tpu as pltpu
from jax.sharding import PartitionSpec as P

MESH = pl.DeviceIdType.MESH
epsilon = 1e-06
bf16 = jnp.bfloat16
f32 = jnp.float32


def kernel(sizes, cap, ids_ref, lev_ref, tok_ref, gain_ref, wg_any, wu_any, wd_any, out_ref,
           wg, wu, wd, meta, meta_nb, meta_prev, meta_pnb, tok_nb, tok_prev, raw, onehot, outb, gat, gains,
           part, rs_opp, rs_l, rs_r, res, ret, cx_out, cx_in, xp_out, xp_in,
           w_sem, disp_s, disp_r, ag_s, ag_r, rs_s, rs_rr, ret_s, ret_r, misc_s, misc_r):
    n_pipe, n_exp, n_dp = sizes
    group = n_exp // 2
    tokens, quarter = tok_ref.shape
    half_rows = group * cap
    chunk = half_rows // 2
    split = chunk // 4
    full_width = n_dp * quarter

    z = lax.axis_index("pipe")
    e = lax.axis_index("expert")
    d = lax.axis_index("dp")
    x_lo = lax.rem(lax.div(e, 2), 2)
    g = lax.div(e, 4) * 2 + lax.rem(e, 2)
    right, left = lax.rem(d + 1, n_dp), lax.rem(d + n_dp - 1, n_dp)
    z_next, z_prev = lax.rem(z + 1, n_pipe), lax.rem(z + n_pipe - 1, n_pipe)

    def member(i):
        return lax.div(i, 2) * 4 + x_lo * 2 + lax.rem(i, 2)

    def offset(s):
        return jnp.where(lax.rem(s, 2) == 1, lax.div(s + 1, 2), group - lax.div(s, 2))

    def ahead(s):
        return member(lax.rem(g + offset(s), group))

    def behind(s):
        return member(lax.rem(g + 2 * group - offset(s), group))

    across = lax.div(e, 4) * 4 + (1 - x_lo) * 2 + lax.rem(e, 2)

    barrier = pltpu.get_barrier_semaphore()

    def tell_group(s, carry):
        pl.semaphore_signal(barrier, inc=1, device_id=(z, ahead(s), d), device_id_type=MESH)
        return carry

    def tell_before(s, carry):
        pl.semaphore_signal(barrier, inc=1, device_id=(z_prev, ahead(s), d), device_id_type=MESH)
        return carry

    pl.semaphore_signal(barrier, inc=1, device_id=(z, across, d), device_id_type=MESH)
    pl.semaphore_signal(barrier, inc=1, device_id=(z, across, right), device_id_type=MESH)
    pl.semaphore_signal(barrier, inc=1, device_id=(z, e, right), device_id_type=MESH)
    pl.semaphore_signal(barrier, inc=1, device_id=(z, e, left), device_id_type=MESH)
    lax.fori_loop(1, group, tell_group, 0)
    lax.fori_loop(0, group, tell_before, 0)

    quarters = [d, left, right, lax.rem(d + 2, n_dp)]
    loads = []
    for q in range(4):
        at = pl.ds(pl.multiple_of(quarters[q] * quarter, 128), quarter)
        loads.append(pltpu.make_async_copy(wg_any.at[at, :], wg.at[q], w_sem.at[3 * q]))
        loads.append(pltpu.make_async_copy(wu_any.at[at, :], wu.at[q], w_sem.at[3 * q + 1]))
        loads.append(pltpu.make_async_copy(wd_any.at[:, at], wd.at[q], w_sem.at[3 * q + 2]))
    for copy in loads:
        copy.start()

    def place(meta_ref):
        i = lax.broadcasted_iota(jnp.int32, (group, tokens), 0)
        off = jnp.where((i & 1) == 1, (i + 1) >> 1, group - (i >> 1))
        member_of = (g + off) & (group - 1)
        expert = (member_of >> 1) * 4 + x_lo * 2 + (member_of & 1)
        first = meta_ref[0:1, :] == expert
        second = meta_ref[1:2, :] == expert
        named = jnp.where(first | second, 1.0, 0.0)
        earlier = lax.broadcasted_iota(jnp.int32, (tokens, tokens), 0) < lax.broadcasted_iota(jnp.int32, (tokens, tokens), 1)
        before = jnp.dot(named.astype(bf16), jnp.where(earlier, 1.0, 0.0).astype(bf16), preferred_element_type=f32)
        rank = jnp.where(named > 0.5, before, 255.0)
        owner = lax.broadcasted_iota(jnp.int32, (half_rows, group), 0) // cap
        spread = jnp.where(owner == lax.broadcasted_iota(jnp.int32, (half_rows, group), 1), 1.0, 0.0).astype(bf16)
        wide = jnp.dot(spread, rank.astype(bf16), preferred_element_type=f32)
        slot = lax.broadcasted_iota(jnp.int32, (half_rows, tokens), 0) & (cap - 1)
        return wide == slot.astype(f32), first, second, spread

    extra, other = (1, 2), (2, 1)

    def kept(h, k):
        return extra[h] if k else 0

    def rc(src, dst, ssem, rsem, device):
        return pltpu.make_async_remote_copy(src_ref=src, dst_ref=dst, send_sem=ssem, recv_sem=rsem, device_id=device, device_id_type=MESH)

    def each(low, high, action):
        def step(s, carry):
            action(s)
            return carry

        lax.fori_loop(low, high, step, 0)

    def route(h, k, token_ref):
        rows = jnp.dot(onehot[h], token_ref[...], preferred_element_type=f32).astype(bf16)
        outb[k, h * half_rows:(h + 1) * half_rows, :] = rows
        gat[kept(h, k), h * half_rows:h * half_rows + cap, :] = rows[0:cap]

    meta[0:2, :] = ids_ref[...]
    meta[2:4, :] = lev_ref[...]
    meta[4:8, :] = jnp.zeros((4, tokens), jnp.int32)
    gains[0] = jnp.broadcast_to(gain_ref[...].astype(f32).reshape(1, quarter), (16, quarter)).astype(bf16)
    onehot[0] = jnp.where(place(meta)[0], 1.0, 0.0).astype(bf16)
    route(0, 0, tok_ref)

    pl.semaphore_wait(barrier, 2 * group + 3)

    nb = (z, across, d)
    to_right, to_left = (z, e, right), (z, e, left)
    to = (None, to_left, to_right)
    copy_meta_nb = rc(meta, meta_nb, misc_s.at[0], misc_r.at[0], nb)
    copy_tok_nb = rc(tok_ref, tok_nb, misc_s.at[1], misc_r.at[1], nb)
    copy_meta_prev = rc(meta, meta_prev, misc_s.at[2], misc_r.at[2], (z_next, e, d))
    copy_tok_prev = rc(tok_ref, tok_prev, misc_s.at[3], misc_r.at[3], (z_next, e, d))
    copy_meta_pnb = rc(meta_prev, meta_pnb, misc_s.at[4], misc_r.at[4], nb)
    copy_gain_r = rc(gains.at[0], gains.at[1], misc_s.at[5], misc_r.at[5], to_right)
    copy_gain_l = rc(gains.at[0], gains.at[2], misc_s.at[6], misc_r.at[6], to_left)
    copy_gain_o = rc(gains.at[1], gains.at[3], misc_s.at[7], misc_r.at[7], to_right)
    copy_part = rc(xp_out, xp_in, misc_s.at[8], misc_r.at[8], nb)
    copy_raw = [rc(tok_ref, raw.at[h], misc_s.at[9 + h], misc_r.at[9 + h], there) for h, there in enumerate((to_right, (z, across, left)))]
    copy_cx = rc(cx_out, cx_in, misc_s.at[11], misc_r.at[11], to[extra[1]])

    def dispatch(h, k, s):
        at = pl.ds(pl.multiple_of(h * half_rows + s * cap, cap), cap)
        sem = (2 * h + k, s)
        return rc(outb.at[k, at, :], gat.at[kept(h, k), at, :], disp_s.at[sem], disp_r.at[sem], (z, ahead(s), d))

    def giving_back(h, k, s):
        at = pl.ds(pl.multiple_of(h * half_rows + s * cap, cap), cap)
        sem = (2 * h + k, s)
        return rc(res.at[k, at, :], ret.at[k, at, :], ret_s.at[sem], ret_r.at[sem], (z_next, behind(s), d))

    chunks = [(0, 0), (1, 0), (1, 1), (0, 1)]
    C00, C10, C11, C01 = 0, 1, 2, 3
    starts = [h * half_rows + p * chunk for h, p in chunks]

    def rows_of(c):
        return pl.ds(starts[c], chunk)

    def upper(c):
        return pl.ds(starts[c], split)

    def lower(c):
        return pl.ds(starts[c] + split, chunk - split)

    def send_rows(c, k):
        h, p = chunks[c]
        each(max(p * (group // 2), 1), (p + 1) * (group // 2), lambda s: dispatch(h, k, s).start())

    def wait_rows(c, k):
        h, p = chunks[c]
        each(max(p * (group // 2), 1), (p + 1) * (group // 2), lambda s: dispatch(h, k, s).wait_recv())

    ag = [
        [
            rc(gat.at[0, rows_of(c), :], gat.at[other[h], rows_of(c), :], ag_s.at[c, 0], ag_r.at[c, 0], to[extra[h]]),
            rc(gat.at[extra[h], rows_of(c), :], gat.at[3, rows_of(c), :], ag_s.at[c, 1], ag_r.at[c, 1], to[other[h]]),
        ]
        for c, (h, _) in enumerate(chunks)
    ]

    def ring(c):
        return chunks[c][0] == 0

    rs = []
    for c, (h, _) in enumerate(chunks):
        if ring(c):
            rs.append([
                rc(part.at[3, upper(c), :], rs_opp.at[upper(c), :], rs_s.at[c, 0], rs_rr.at[c, 0], to_right),
                rc(part.at[3, lower(c), :], rs_opp.at[lower(c), :], rs_s.at[c, 1], rs_rr.at[c, 1], to_left),
                rc(part.at[2, rows_of(c), :], rs_l.at[rows_of(c), :], rs_s.at[c, 2], rs_rr.at[c, 2], to_right),
                rc(part.at[1, rows_of(c), :], rs_r.at[rows_of(c), :], rs_s.at[c, 3], rs_rr.at[c, 3], to_left),
            ])
        else:
            rs.append([
                rc(part.at[3, rows_of(c), :], rs_l.at[rows_of(c), :], rs_s.at[c, 0], rs_rr.at[c, 0], to[extra[h]]),
                rc(part.at[other[h], rows_of(c), :], rs_r.at[rows_of(c), :], rs_s.at[c, 1], rs_rr.at[c, 1], to[other[h]]),
            ])

    def compute(c):
        h, _ = chunks[c]
        at = rows_of(c)
        gate = jnp.zeros((chunk, wg.shape[2]), f32)
        up = jnp.zeros((chunk, wg.shape[2]), f32)
        squares = jnp.zeros((chunk, 1), f32)
        for q in (0, extra[h], other[h], 3):
            if q == other[h]:
                ag[c][0].wait_recv()
            if q == 3:
                ag[c][1].wait_recv()
            wide = gat[q, at, :].astype(f32)
            squares = squares + jnp.sum(wide * wide, axis=1, keepdims=True)
            scaled = (wide * gains[q, 0:1, :].astype(f32)).astype(bf16)
            gate = gate + jnp.dot(scaled, wg[q], preferred_element_type=f32)
            up = up + jnp.dot(scaled, wu[q], preferred_element_type=f32)
        inverse = lax.rsqrt(squares / full_width + epsilon)
        gate = inverse * gate
        up = inverse * up
        hidden = (gate / (1.0 + jnp.exp(-gate)) * up).astype(bf16)
        for q in (3, other[h], extra[h], 0):
            part[q, at, :] = jnp.dot(hidden, wd[q], preferred_element_type=f32).astype(bf16)
            if q == 3:
                rs[c][0].start()
                if ring(c):
                    rs[c][1].start()
            if q == other[h] and not ring(c):
                rs[c][1].start()

    def reduce_on(c):
        rs[c][0].wait_recv()
        at = upper(c)
        part[2, at, :] = (part[2, at, :].astype(f32) + rs_opp[at, :].astype(f32)).astype(bf16)
        rs[c][2].start()
        rs[c][1].wait_recv()
        at = lower(c)
        part[1, at, :] = (part[1, at, :].astype(f32) + rs_opp[at, :].astype(f32)).astype(bf16)
        rs[c][3].start()

    def give_back(c, k):
        h, p = chunks[c]
        at = rows_of(c)
        if ring(c):
            rs[c][2].wait_recv()
            rs[c][3].wait_recv()
            total = part[0, at, :].astype(f32) + rs_l[at, :].astype(f32) + rs_r[at, :].astype(f32)
        elif k:
            rs[c][0].wait_recv()
            total = part[extra[h], at, :].astype(f32) + rs_l[at, :].astype(f32)
        else:
            rs[c][1].wait_recv()
            total = part[0, at, :].astype(f32) + rs_r[at, :].astype(f32)
        res[k, at, :] = total.astype(bf16)
        each(p * (group // 2), (p + 1) * (group // 2), lambda s: giving_back(h, k, s).start())

    def weights(meta_ref):
        placed, first, second, spread = place(meta_ref)
        levels = meta_ref[2:4, :].astype(f32)
        total = levels[0:1] + levels[1:2]
        share = jnp.where(first, levels[0:1] / total, jnp.where(second, levels[1:2] / total, 0.0))
        high = share.astype(bf16)
        low = (share - high.astype(f32)).astype(bf16)
        return [jnp.where(placed, jnp.dot(spread, piece, preferred_element_type=f32), 0.0).astype(bf16) for piece in (high, low)]

    def combine(pieces, h, k):
        each(0, group, lambda s: giving_back(h, k, s).wait_recv())
        acc = jnp.zeros((tokens, quarter), f32)
        for piece in pieces:
            acc = acc + lax.dot_general(
                piece, ret[k, h * half_rows:(h + 1) * half_rows, :], (((0,), (0,)), ((), ())), preferred_element_type=f32
            )
        return acc

    copy_meta_nb.start()
    copy_tok_nb.start()
    copy_raw[0].start()
    copy_raw[1].start()
    send_rows(C00, 0)
    copy_gain_r.start()
    copy_gain_l.start()
    copy_meta_prev.start()
    copy_meta_nb.wait_recv()
    onehot[1] = jnp.where(place(meta_nb)[0], 1.0, 0.0).astype(bf16)
    copy_tok_nb.wait_recv()
    route(1, 0, tok_nb)
    send_rows(C10, 0)
    wait_rows(C00, 0)
    ag[C00][0].start()
    copy_raw[0].wait_recv()
    route(0, 1, raw.at[0])
    send_rows(C00, 1)
    copy_raw[1].wait_recv()
    route(1, 1, raw.at[1])
    send_rows(C10, 1)
    send_rows(C01, 0)
    send_rows(C11, 0)
    send_rows(C01, 1)
    send_rows(C11, 1)
    wait_rows(C10, 0)
    ag[C10][0].start()
    copy_gain_r.wait_recv()
    copy_gain_o.start()
    wait_rows(C00, 1)
    ag[C00][1].start()
    wait_rows(C10, 1)
    ag[C10][1].start()
    copy_meta_prev.wait_recv()
    copy_meta_pnb.start()
    for copy in loads:
        copy.wait()
    copy_gain_l.wait_recv()
    copy_gain_o.wait_recv()
    wait_rows(C01, 0)
    ag[C01][0].start()
    wait_rows(C11, 0)
    ag[C11][0].start()
    compute(C00)
    wait_rows(C01, 1)
    ag[C01][1].start()
    compute(C10)
    wait_rows(C11, 1)
    ag[C11][1].start()
    copy_tok_prev.start()
    reduce_on(C00)
    copy_meta_pnb.wait_recv()
    compute(C11)
    compute(C01)
    give_back(C10, 1)
    give_back(C10, 0)
    give_back(C00, 0)
    give_back(C11, 1)
    give_back(C11, 0)
    reduce_on(C01)
    pieces = weights(meta_pnb)
    cx_out[...] = combine(pieces, 1, 1).astype(bf16)
    copy_cx.start()
    theirs = combine(pieces, 1, 0)
    give_back(C01, 0)
    copy_cx.wait_recv()
    xp_out[...] = (theirs + cx_in[...].astype(f32)).astype(bf16)
    copy_part.start()
    copy_tok_prev.wait_recv()
    mine = combine(weights(meta_prev), 0, 0)
    copy_part.wait_recv()
    out_ref[...] = (tok_prev[...].astype(f32) + (mine + xp_in[...].astype(f32))).astype(bf16)

    for copy in (copy_meta_nb, copy_tok_nb, copy_meta_prev, copy_tok_prev, copy_meta_pnb, copy_gain_r, copy_gain_l, copy_gain_o, copy_part, copy_cx, *copy_raw):
        copy.wait_send()
    for c in range(4):
        for copy in (*ag[c], *rs[c]):
            copy.wait_send()
    for h in range(2):
        for k in range(2):
            each(1, group, lambda s: dispatch(h, k, s).wait_send())
            if k == 0 or h == 1:
                each(0, group, lambda s: giving_back(h, k, s).wait_send())


def body(sizes, interpret, tokens, expert_ids, gate_levels, gain, w_gate, w_up, w_down):
    rows, quarter = tokens.shape[1:]
    fanout = expert_ids.shape[2]
    n_exp = sizes[1]
    cap = min(rows, max(2, 2 * rows * fanout // n_exp))
    group = n_exp // 2
    every = 2 * group * cap
    ff = w_gate.shape[2]
    vmem = pl.BlockSpec(memory_space=pltpu.VMEM)
    anywhere = pl.BlockSpec(memory_space=pl.ANY)
    dma = pltpu.SemaphoreType.DMA
    out = pl.pallas_call(
        functools.partial(kernel, sizes, cap),
        out_shape=jax.ShapeDtypeStruct((rows, quarter), bf16),
        in_specs=[vmem, vmem, vmem, vmem, anywhere, anywhere, anywhere],
        out_specs=vmem,
        scratch_shapes=[
            pltpu.VMEM((4, quarter, ff), bf16),
            pltpu.VMEM((4, quarter, ff), bf16),
            pltpu.VMEM((4, ff, quarter), bf16),
            *[pltpu.VMEM((8, rows), jnp.int32)] * 4,
            *[pltpu.VMEM((rows, quarter), bf16)] * 2,
            pltpu.VMEM((2, rows, quarter), bf16),
            pltpu.VMEM((2, group * cap, rows), bf16),
            pltpu.VMEM((2, every, quarter), bf16),
            pltpu.VMEM((4, every, quarter), bf16),
            pltpu.VMEM((4, 16, quarter), bf16),
            pltpu.VMEM((4, every, quarter), bf16),
            *[pltpu.VMEM((every, quarter), bf16)] * 3,
            *[pltpu.VMEM((2, every, quarter), bf16)] * 2,
            *[pltpu.VMEM((rows, quarter), bf16)] * 4,
            dma((12,)),
            dma((4, group)),
            dma((4, group)),
            *[dma((4, 2))] * 2,
            *[dma((4, 4))] * 2,
            dma((4, group)),
            dma((4, group)),
            dma((12,)),
            dma((12,)),
        ],
        compiler_params=pltpu.CompilerParams(collective_id=0, has_side_effects=True, vmem_limit_bytes=61 * 1024 * 1024),
        interpret=interpret,
    )(expert_ids[0].T, gate_levels[0].T, tokens[0], gain, w_gate[0], w_up[0], w_down[0])
    return out[None]


def solution(mesh, interpret=False):
    sizes = (mesh.shape["pipe"], mesh.shape["expert"], mesh.shape["dp"])
    return jax.shard_map(
        functools.partial(body, sizes, interpret),
        mesh=mesh,
        in_specs=(
            P("pipe", "expert", "dp"),
            P("pipe", "expert", None),
            P("pipe", "expert", None),
            P("dp"),
            P("expert", None, "dp"),
            P("expert", None, "dp"),
            P("expert", "dp", None),
        ),
        out_specs=P("pipe", "expert", "dp"),
        check_vma=False,
    )
```

time: 179 us -> 161 us (0.90)
  the two profiles are of different devices: /device:TPU:6 before, /device:TPU:98 now
where the time goes in v2:
time: 161 us; the launch traced here: 160 us
  Pallas kernels  159 us (99%)
  local copies, waits for them, and re-layouts  1.65 us (1%)
    pallas_call x1, Pallas kernels, body(): pl.pallas_call(functools.partial(kernel, sizes, cap), out_shape=jax.Shape...  159 us

profile of v2, /device:TPU:98, one launch (start us, length us, event | category | flops | bytes accessed | tf_op | source)
XLA Modules:
  0.0 160.4 jit_solution(1552804567732862258)
XLA Ops:
  0.0 158.8 %shard_map.73 = bf16[128,896]{1,0:T(8,128)(2,1)} custom-call(s32[2,128]{1,0:T(2,128)} %bitcast.16, s32[2,128]{1,0:T(2,128)} %bitcast.17, bf16[128,896]{1,0:T(8,128)(2,1)} %bitcast.15, bf16[896]{0:T(1024)(128)(2,1)} %gain_ref.1, bf16[3584,256]{1,0:T(8,128)(2,1)} %bitcast.11, bf16[3584,256]{1,0:T(8,128)(2,1)} %bitcast.12, bf16[256,3584]{1,0:T(8,128)(2,1)} %bitcast.13), custom_call_target="tpu_custom_call" | custom-call | tf_op jit(solution)/shard_map/pallas_call | solution.py:364
  158.8 1.6 %copy.9 = bf16[1,128,896]{2,1,0:T(8,128)(2,1)} copy(bf16[1,128,896]{2,1,0:T(8,128)(2,1)} %bitcast.14) | data formatting | bytes 458752

commit v3 on v2

--- a/solution.py
+++ b/solution.py
@@ -14,7 +14,7 @@
 
 
 def kernel(sizes, cap, ids_ref, lev_ref, tok_ref, gain_ref, wg_any, wu_any, wd_any, out_ref,
-           wg, wu, wd, meta, meta_nb, meta_prev, meta_pnb, tok_nb, tok_prev, raw, onehot, outb, gat, gains,
+           wg, wu, wd, meta, meta_nb, meta_prev, meta_pnb, tok_nb, tok_prev, raw, onehot, shares, outb, gat, gains,
            part, rs_opp, rs_l, rs_r, res, ret, cx_out, cx_in, xp_out, xp_in,
            w_sem, disp_s, disp_r, ag_s, ag_r, rs_s, rs_rr, ret_s, ret_r, misc_s, misc_r):
     n_pipe, n_exp, n_dp = sizes
@@ -247,21 +247,22 @@
         res[k, at, :] = total.astype(bf16)
         each(p * (group // 2), (p + 1) * (group // 2), lambda s: giving_back(h, k, s).start())
 
-    def weights(meta_ref):
+    def share(meta_ref, h):
         placed, first, second, spread = place(meta_ref)
         levels = meta_ref[2:4, :].astype(f32)
         total = levels[0:1] + levels[1:2]
-        share = jnp.where(first, levels[0:1] / total, jnp.where(second, levels[1:2] / total, 0.0))
-        high = share.astype(bf16)
-        low = (share - high.astype(f32)).astype(bf16)
-        return [jnp.where(placed, jnp.dot(spread, piece, preferred_element_type=f32), 0.0).astype(bf16) for piece in (high, low)]
-
-    def combine(pieces, h, k):
+        part_of = jnp.where(first, levels[0:1] / total, jnp.where(second, levels[1:2] / total, 0.0))
+        high = part_of.astype(bf16)
+        low = (part_of - high.astype(f32)).astype(bf16)
+        for i, term in enumerate((high, low)):
+            shares[2 * h + i] = jnp.where(placed, jnp.dot(spread, term, preferred_element_type=f32), 0.0).astype(bf16)
+
+    def combine(h, k):
         each(0, group, lambda s: giving_back(h, k, s).wait_recv())
         acc = jnp.zeros((tokens, quarter), f32)
-        for piece in pieces:
+        for i in range(2):
             acc = acc + lax.dot_general(
-                piece, ret[k, h * half_rows:(h + 1) * half_rows, :], (((0,), (0,)), ((), ())), preferred_element_type=f32
+                shares[2 * h + i], ret[k, h * half_rows:(h + 1) * half_rows, :], (((0,), (0,)), ((), ())), preferred_element_type=f32
             )
         return acc
 
@@ -316,25 +317,26 @@
     ag[C11][1].start()
     copy_tok_prev.start()
     reduce_on(C00)
-    copy_meta_pnb.wait_recv()
     compute(C11)
-    compute(C01)
     give_back(C10, 1)
     give_back(C10, 0)
+    compute(C01)
+    share(meta_prev, 0)
+    copy_meta_pnb.wait_recv()
+    share(meta_pnb, 1)
     give_back(C00, 0)
     give_back(C11, 1)
+    reduce_on(C01)
     give_back(C11, 0)
-    reduce_on(C01)
-    pieces = weights(meta_pnb)
-    cx_out[...] = combine(pieces, 1, 1).astype(bf16)
+    give_back(C01, 0)
+    cx_out[...] = combine(1, 1).astype(bf16)
     copy_cx.start()
-    theirs = combine(pieces, 1, 0)
-    give_back(C01, 0)
+    theirs = combine(1, 0)
     copy_cx.wait_recv()
     xp_out[...] = (theirs + cx_in[...].astype(f32)).astype(bf16)
     copy_part.start()
     copy_tok_prev.wait_recv()
-    mine = combine(weights(meta_prev), 0, 0)
+    mine = combine(0, 0)
     copy_part.wait_recv()
     out_ref[...] = (tok_prev[...].astype(f32) + (mine + xp_in[...].astype(f32))).astype(bf16)
 
@@ -374,6 +376,7 @@
             *[pltpu.VMEM((rows, quarter), bf16)] * 2,
             pltpu.VMEM((2, rows, quarter), bf16),
             pltpu.VMEM((2, group * cap, rows), bf16),
+            pltpu.VMEM((4, group * cap, rows), bf16),
             pltpu.VMEM((2, every, quarter), bf16),
             pltpu.VMEM((4, every, quarter), bf16),
             pltpu.VMEM((4, 16, quarter), bf16),

time: 161 us -> 158 us (0.981)
  the two profiles are of different devices: /device:TPU:98 before, /device:TPU:2 now
where the time goes in v3:
time: 158 us; the launch traced here: 157 us
  Pallas kernels  156 us (99%)
  local copies, waits for them, and re-layouts  1.65 us (1%)
    pallas_call x1, Pallas kernels, body(): pl.pallas_call(functools.partial(kernel, sizes, cap), out_shape=jax.Shape...  156 us

profile of v3, /device:TPU:2, one launch (start us, length us, event | category | flops | bytes accessed | tf_op | source)
XLA Modules:
  0.0 157.3 jit_solution(9018754046064360242)
XLA Ops:
  0.0 155.6 %shard_map.73 = bf16[128,896]{1,0:T(8,128)(2,1)} custom-call(s32[2,128]{1,0:T(2,128)} %bitcast.16, s32[2,128]{1,0:T(2,128)} %bitcast.17, bf16[128,896]{1,0:T(8,128)(2,1)} %bitcast.15, bf16[896]{0:T(1024)(128)(2,1)} %gain_ref.1, bf16[3584,256]{1,0:T(8,128)(2,1)} %bitcast.11, bf16[3584,256]{1,0:T(8,128)(2,1)} %bitcast.12, bf16[256,3584]{1,0:T(8,128)(2,1)} %bitcast.13), custom_call_target="tpu_custom_call" | custom-call | tf_op jit(solution)/shard_map/pallas_call | solution.py:366
  155.6 1.6 %copy.9 = bf16[1,128,896]{2,1,0:T(8,128)(2,1)} copy(bf16[1,128,896]{2,1,0:T(8,128)(2,1)} %bitcast.14) | data formatting | bytes 458752
